TPU v7x, 32 devices: a whole 2x2x4 slice. The times are simulated.
32 devices in a mesh: dp: 8 (over z, x), tensor: 4 (over y, core).
Axes of the slice: x: 2, y: 2, z: 4, core: 2. Of those that a mesh axis runs over, the one named last changes fastest.
Arguments:
- block_input: bfloat16 [8192, 768], P(('dp', 'tensor')), may hold values from -6 to 6
- out_cotangent: bfloat16 [8192, 768], P(('dp', 'tensor')), may hold values from -6 to 6
- seq_lengths: int32 [8, 4], replicated, may hold values from 1 to 682, 1024 in all within a row
- pack_order: int32 [8], replicated, may hold values from 0 to 7, each once
- ln1_gain: float32 [768], replicated, may hold values from 0.5 to 1.5
- ln1_bias: float32 [768], replicated, may hold values from -1.5 to 1.5
- qkv_weight: float32 [768, 3, 768], P('dp', None, 'tensor'), may hold values from -0.21875 to 0.21875
- qv_bias: float32 [2, 768], P(None, 'tensor'), may hold values from -1.5 to 1.5
- attn_out_weight: float32 [768, 768], P('tensor', 'dp'), may hold values from -1.75 to 1.75
- attn_out_bias: float32 [768], replicated, may hold values from -1.5 to 1.5
- ln2_gain: float32 [768], replicated, may hold values from 0.5 to 1.5
- ln2_bias: float32 [768], replicated, may hold values from -1.5 to 1.5
- fc_weight: float32 [768, 3072], P('dp', 'tensor'), may hold values from -0.21875 to 0.21875
- fc_bias: float32 [3072], P('tensor'), may hold values from -1.5 to 1.5
- proj_weight: float32 [3072, 768], P('tensor', 'dp'), may hold values from -0.109375 to 0.109375
- proj_bias: float32 [768], replicated, may hold values from -1.5 to 1.5
Outputs:
- block_output: bfloat16 [8192, 768], P(('dp', 'tensor'))
- input_grad: bfloat16 [8192, 768], P(('dp', 'tensor'))
- ln1_gain_grad: float32 [768], replicated
- ln1_bias_grad: float32 [768], replicated
- qkv_weight_grad: float32 [768, 3, 768], P('dp', None, 'tensor')
- qv_bias_grad: float32 [2, 768], P(None, 'tensor')
- attn_out_weight_grad: float32 [768, 768], P('tensor', 'dp')
- attn_out_bias_grad: float32 [768], replicated
- ln2_gain_grad: float32 [768], replicated
- ln2_bias_grad: float32 [768], replicated
- fc_weight_grad: float32 [768, 3072], P('dp', 'tensor')
- fc_bias_grad: float32 [3072], P('tensor')
- proj_weight_grad: float32 [3072, 768], P('tensor', 'dp')
- proj_bias_grad: float32 [768], replicated
Inputs may be any that keep to these rules, and one draw needn't show every extreme that they name: `seq_lengths`: each row gives the lengths of the 4 sequences of one pack in order, sums to 1024, and its largest entry is 682. `pack_order`: a permutation of the 8 packs.
All inputs are finite; a program needn't handle non-finite values.
Results may differ from a plain program's by a relative error of at most 0.017.
Values may be sent and summed in bfloat16 or wider, within the bound.
A program may use at most 128 MiB of HBM per device.

v0:
```python
import jax
import jax.numpy as jnp
from jax import lax
from jax.sharding import PartitionSpec as P

HEAD_DIM = 64
EPSILON = 1e-05
MASKED = -1e30


def gelu_curve(values):
    return (
        0.5
        * values
        * (1.0 + jnp.tanh(0.7978845608028654 * (values + 0.044715 * values * values * values)))
    )


def contract(left_side, right_side, left_dim, right_dim):
    return lax.dot_general(
        left_side,
        right_side,
        (((left_dim,), (right_dim,)), ((), ())),
        preferred_element_type=jnp.float32,
    )


def normalize(rows_in, norm_gain, norm_bias):
    row_mean = jnp.mean(rows_in, axis=1, keepdims=True)
    row_var = jnp.mean(rows_in * rows_in, axis=1, keepdims=True) - row_mean * row_mean
    row_scale = lax.rsqrt(row_var + EPSILON)
    centered = (rows_in - row_mean) * row_scale
    return (centered, row_scale, (centered * norm_gain + norm_bias).astype(jnp.bfloat16))


def norm_back(grad_in, centered, row_scale, norm_gain):
    gain_grad = jnp.sum(grad_in * centered, axis=0)
    bias_grad = jnp.sum(grad_in, axis=0)
    scaled = grad_in * norm_gain
    back = row_scale * (
        scaled
        - jnp.mean(scaled, axis=1, keepdims=True)
        - centered * jnp.mean(scaled * centered, axis=1, keepdims=True)
    )
    return (back, gain_grad, bias_grad)


def grad_rows(local_rows):
    return lax.all_gather(local_rows, "tensor", axis=0, tiled=True)


def input_total(partial_value):
    return lax.psum_scatter(
        partial_value.astype(jnp.bfloat16), "tensor", scatter_dimension=0, tiled=True
    ).astype(jnp.float32)


def block_scores(query_rows, keys_seen, segment, begin_row):
    block_len = query_rows.shape[0]
    key_count = keys_seen.shape[0]
    row_pos = begin_row + jnp.arange(block_len, dtype=jnp.int32)
    col_pos = jnp.arange(key_count, dtype=jnp.int32)
    row_segment = segment[begin_row : begin_row + block_len]
    allowed = (col_pos[None, :] <= row_pos[:, None]) & (
        segment[None, :key_count] == row_segment[:, None]
    )
    raw_scores = jnp.einsum(
        "qhd,khd->hqk", query_rows, keys_seen, preferred_element_type=jnp.float32
    ) * query_rows.shape[2] ** (-0.5)
    return jnp.where(allowed[None], raw_scores, MASKED)


def attend(queries, keys_all, values_all, segment, block_len):
    outputs = []
    log_totals = []
    for begin_row in range(0, queries.shape[0], block_len):
        final_row = begin_row + block_len
        query_rows = queries[begin_row:final_row]
        scores = block_scores(query_rows, keys_all[:final_row], segment, begin_row)
        row_peak = jnp.max(scores, axis=-1, keepdims=True)
        weights = jnp.exp(scores - row_peak)
        weight_total = jnp.sum(weights, axis=-1, keepdims=True)
        probs = (weights / weight_total).astype(jnp.bfloat16)
        outputs.append(
            jnp.einsum(
                "hqk,khd->qhd", probs, values_all[:final_row], preferred_element_type=jnp.float32
            )
        )
        log_totals.append(row_peak + jnp.log(weight_total))
    return (jnp.concatenate(outputs, axis=0), log_totals)


def attend_back(queries, keys_all, values_all, segment, block_len, log_totals, out_grad):
    factor = queries.shape[2] ** (-0.5)
    key_grad = jnp.zeros(keys_all.shape, jnp.float32)
    value_grad = jnp.zeros(values_all.shape, jnp.float32)
    query_grads = []
    for block_index, begin_row in enumerate(range(0, queries.shape[0], block_len)):
        final_row = begin_row + block_len
        query_rows = queries[begin_row:final_row]
        keys_seen = keys_all[:final_row]
        values_seen = values_all[:final_row]
        grad_block = out_grad[begin_row:final_row]
        probs = jnp.exp(
            block_scores(query_rows, keys_seen, segment, begin_row) - log_totals[block_index]
        )
        value_grad = value_grad.at[:final_row].add(
            jnp.einsum(
                "hqk,qhd->khd",
                probs.astype(jnp.bfloat16),
                grad_block,
                preferred_element_type=jnp.float32,
            )
        )
        prob_grad = jnp.einsum(
            "qhd,khd->hqk", grad_block, values_seen, preferred_element_type=jnp.float32
        )
        row_delta = jnp.sum(probs * prob_grad, axis=-1, keepdims=True)
        score_grad = (probs * (prob_grad - row_delta)).astype(jnp.bfloat16)
        query_grads.append(
            jnp.einsum("hqk,khd->qhd", score_grad, keys_seen, preferred_element_type=jnp.float32)
            * factor
        )
        key_grad = key_grad.at[:final_row].add(
            jnp.einsum("hqk,qhd->khd", score_grad, query_rows, preferred_element_type=jnp.float32)
            * factor
        )
    return (jnp.concatenate(query_grads, axis=0), key_grad, value_grad)


def local(
    block_input,
    out_cotangent,
    seq_lengths,
    pack_order,
    ln1_gain,
    ln1_bias,
    qkv_weight,
    qv_bias,
    attn_out_weight,
    attn_out_bias,
    ln2_gain,
    ln2_bias,
    fc_weight,
    fc_bias,
    proj_weight,
    proj_bias,
):
    local_rows, width = block_input.shape
    pack_count = pack_order.shape[0]
    piece_rows = local_rows // pack_count
    pack_rows = local_rows * lax.axis_size("tensor")
    head_cols = qv_bias.shape[1]
    heads_here = head_cols // HEAD_DIM
    block_len = min(512, pack_rows)
    slots = jnp.arange(pack_count, dtype=jnp.int32)
    inverse = jnp.sum(jnp.where(pack_order[None, :] == slots[:, None], slots[None, :], 0), axis=1)
    sent_input = jnp.take(
        block_input.reshape(pack_count, piece_rows, width), inverse, axis=0
    ).reshape(local_rows, width)
    sent_grad = jnp.take(
        out_cotangent.reshape(pack_count, piece_rows, width), inverse, axis=0
    ).reshape(local_rows, width)
    arrived = (
        lax.all_to_all(sent_input, "dp", split_axis=0, concat_axis=0, tiled=True),
        lax.all_to_all(sent_grad, "dp", split_axis=0, concat_axis=0, tiled=True),
    )
    input_here = arrived[0].astype(jnp.float32)
    grad_here = arrived[1].astype(jnp.float32)
    my_pack = lax.axis_index("dp")
    my_lengths = lax.dynamic_index_in_dim(seq_lengths, my_pack, 0, keepdims=False)
    seq_ends = jnp.cumsum(my_lengths)
    positions = jnp.arange(pack_rows, dtype=jnp.int32)
    segment = jnp.sum((positions[:, None] >= seq_ends[None, :]).astype(jnp.int32), axis=1)
    weights = (
        lax.all_gather(qkv_weight.astype(jnp.bfloat16), "dp", axis=0, tiled=True),
        lax.all_gather(attn_out_weight.astype(jnp.bfloat16), "dp", axis=1, tiled=True),
        lax.all_gather(fc_weight.astype(jnp.bfloat16), "dp", axis=0, tiled=True),
        lax.all_gather(proj_weight.astype(jnp.bfloat16), "dp", axis=1, tiled=True),
    )
    qkv_full = weights[0].reshape(width, 3 * head_cols)
    out_full = weights[1]
    fc_full = weights[2]
    proj_full = weights[3]
    centered_one, scale_one, ln_one = normalize(input_here, ln1_gain, ln1_bias)
    normed_one = lax.all_gather(ln_one, "tensor", axis=0, tiled=True)
    projected = jnp.dot(normed_one, qkv_full, preferred_element_type=jnp.float32)
    queries = (
        (projected[:, :head_cols] + qv_bias[0])
        .astype(jnp.bfloat16)
        .reshape(pack_rows, heads_here, HEAD_DIM)
    )
    keys_all = (
        projected[:, head_cols : 2 * head_cols]
        .astype(jnp.bfloat16)
        .reshape(pack_rows, heads_here, HEAD_DIM)
    )
    values_all = (
        (projected[:, 2 * head_cols :] + qv_bias[1])
        .astype(jnp.bfloat16)
        .reshape(pack_rows, heads_here, HEAD_DIM)
    )
    attended, log_totals = attend(queries, keys_all, values_all, segment, block_len)
    attended_low = attended.reshape(pack_rows, head_cols).astype(jnp.bfloat16)
    attn_partial = jnp.dot(attended_low, out_full, preferred_element_type=jnp.float32)
    attn_here = lax.psum_scatter(
        attn_partial.astype(jnp.bfloat16), "tensor", scatter_dimension=0, tiled=True
    ).astype(jnp.float32)
    resid_one = input_here + attn_here + attn_out_bias
    centered_two, scale_two, ln_two = normalize(resid_one, ln2_gain, ln2_bias)
    normed_two = lax.all_gather(ln_two, "tensor", axis=0, tiled=True)
    upper_pre = jnp.dot(normed_two, fc_full, preferred_element_type=jnp.float32) + fc_bias
    activated = gelu_curve(upper_pre).astype(jnp.bfloat16)
    mlp_here = lax.psum_scatter(
        jnp.dot(activated, proj_full, preferred_element_type=jnp.float32).astype(jnp.bfloat16),
        "tensor",
        scatter_dimension=0,
        tiled=True,
    ).astype(jnp.float32)
    block_output = (resid_one + mlp_here + proj_bias).astype(jnp.bfloat16)
    proj_bias_grad = jnp.sum(grad_here, axis=0)
    mlp_grad = grad_rows(grad_here.astype(jnp.bfloat16))
    proj_grad = contract(activated, mlp_grad, 0, 0)
    act_grad = contract(mlp_grad, proj_full, 1, 1)
    gelu_pull = jax.vjp(gelu_curve, upper_pre)[1]
    upper_grad = gelu_pull(act_grad)[0].astype(jnp.bfloat16)
    fc_bias_grad = jnp.sum(upper_grad.astype(jnp.float32), axis=0)
    fc_grad = contract(normed_two, upper_grad, 0, 0)
    normed_two_grad = input_total(contract(upper_grad, fc_full, 1, 1))
    back_two, ln2_gain_grad, ln2_bias_grad = norm_back(
        normed_two_grad, centered_two, scale_two, ln2_gain
    )
    resid_grad = grad_here + back_two
    attn_out_bias_grad = jnp.sum(resid_grad, axis=0)
    attn_grad_rows = grad_rows(resid_grad.astype(jnp.bfloat16))
    out_weight_grad = contract(attended_low, attn_grad_rows, 0, 0)
    attended_grad = (
        contract(attn_grad_rows, out_full, 1, 1)
        .astype(jnp.bfloat16)
        .reshape(pack_rows, heads_here, HEAD_DIM)
    )
    query_grad, key_grad, value_grad = attend_back(
        queries, keys_all, values_all, segment, block_len, log_totals, attended_grad
    )
    query_low = query_grad.reshape(pack_rows, head_cols).astype(jnp.bfloat16)
    key_low = key_grad.reshape(pack_rows, head_cols).astype(jnp.bfloat16)
    value_low = value_grad.reshape(pack_rows, head_cols).astype(jnp.bfloat16)
    qv_bias_grad = jnp.stack(
        [
            jnp.sum(query_low.astype(jnp.float32), axis=0),
            jnp.sum(value_low.astype(jnp.float32), axis=0),
        ]
    )
    joined_grad = jnp.concatenate([query_low, key_low, value_low], axis=1)
    qkv_grad = contract(normed_one, joined_grad, 0, 0).reshape(width, 3, head_cols)
    normed_one_grad = input_total(contract(joined_grad, qkv_full, 1, 1))
    back_one, ln1_gain_grad, ln1_bias_grad = norm_back(
        normed_one_grad, centered_one, scale_one, ln1_gain
    )
    input_grad = (resid_grad + back_one).astype(jnp.bfloat16)
    returned = (
        lax.all_to_all(block_output, "dp", split_axis=0, concat_axis=0, tiled=True),
        lax.all_to_all(input_grad, "dp", split_axis=0, concat_axis=0, tiled=True),
    )
    out_rows = jnp.take(
        returned[0].reshape(pack_count, piece_rows, width), pack_order, axis=0
    ).reshape(local_rows, width)
    grad_out_rows = jnp.take(
        returned[1].reshape(pack_count, piece_rows, width), pack_order, axis=0
    ).reshape(local_rows, width)
    all_sums = (
        lax.psum_scatter(qkv_grad, "dp", scatter_dimension=0, tiled=True),
        lax.psum_scatter(out_weight_grad, "dp", scatter_dimension=1, tiled=True),
        lax.psum_scatter(fc_grad, "dp", scatter_dimension=0, tiled=True),
        lax.psum_scatter(proj_grad, "dp", scatter_dimension=1, tiled=True),
    )
    qkv_sum, out_sum, fc_sum, proj_sum = (all_sums[0], all_sums[1], all_sums[2], all_sums[3])
    head_sums = lax.psum((qv_bias_grad, fc_bias_grad), "dp")
    shared_sums = lax.psum(
        (
            ln1_gain_grad,
            ln1_bias_grad,
            attn_out_bias_grad,
            ln2_gain_grad,
            ln2_bias_grad,
            proj_bias_grad,
        ),
        ("dp", "tensor"),
    )
    return (
        out_rows,
        grad_out_rows,
        shared_sums[0],
        shared_sums[1],
        qkv_sum,
        head_sums[0],
        out_sum,
        shared_sums[2],
        shared_sums[3],
        shared_sums[4],
        fc_sum,
        head_sums[1],
        proj_sum,
        shared_sums[5],
    )


def solution(mesh):
    return jax.shard_map(
        local,
        mesh=mesh,
        in_specs=(
            P(("dp", "tensor"), None),
            P(("dp", "tensor"), None),
            P(),
            P(),
            P(),
            P(),
            P("dp", None, "tensor"),
            P(None, "tensor"),
            P("tensor", "dp"),
            P(),
            P(),
            P(),
            P("dp", "tensor"),
            P("tensor"),
            P("tensor", "dp"),
            P(),
        ),
        out_specs=(
            P(("dp", "tensor"), None),
            P(("dp", "tensor"), None),
            P(),
            P(),
            P("dp", None, "tensor"),
            P(None, "tensor"),
            P("tensor", "dp"),
            P(),
            P(),
            P(),
            P("dp", "tensor"),
            P("tensor"),
            P("tensor", "dp"),
            P(),
        ),
        check_vma=False,
    )
```

profile of v0, /device:TPU:0, one launch (start us, length us, event | category | flops | bytes accessed | tf_op | source)
XLA Modules:
  0.0 679.9 jit_solution(4538594426250467787)
XLA Ops:
  8.1 0.9 select_reduce_fusion
  9.6 1.6 gather_fusion
  11.2 0.9 broadcast_select_fusion.2
  12.1 19.1 %all_to_all.33 = bf16[8,32,768]{2,1,0:T(8,128)(2,1)S(1)} all-to-all(bf16[8,32,768]{2,1,0:T(8,128)(2,1)S(1)} %get-tuple-element.121), channel_id=1, replica_groups=mesh['dp'=8,'tensor'=4] {'dp'}, dimensions={0} | all-to-all | bytes 786432 | tf_op jit(solution)/shard_map/all_to_all | solution.py:165
  31.6 1.0 fusion.66
  33.3 36.0 %all_gather.25 = bf16[768,3,192]{2,1,0:T(4,128)(2,1)S(1)} all-gather(bf16[96,3,192]{2,1,0:T(4,128)(2,1)S(1)} %copy.57), channel_id=1, replica_groups=mesh['dp'=8,'tensor'=4] {'dp'}, dimensions={0}, use_global_device_ids=true | all-gather | bytes 995328 | tf_op jit(solution)/shard_map/all_gather | solution.py:176
  69.3 0.9 copy.58
  70.3 33.0 %all_gather.26 = bf16[192,768]{0,1:T(8,128)(2,1)} all-gather(bf16[192,96]{0,1:T(8,128)(2,1)S(1)} %copy.60), channel_id=1, replica_groups=mesh['dp'=8,'tensor'=4] {'dp'}, dimensions={1}, use_global_device_ids=true | all-gather | bytes 331776 | tf_op jit(solution)/shard_map/all_gather | solution.py:177
  103.3 0.9 fusion.47
  104.3 1.3 fusion.14
  105.5 2.5 fusion.80
  109.1 0.8 fusion.82
  111.4 1.4 fusion.81
  112.9 1.5 fusion
  114.4 1.1 copy-done.2
  115.5 1.7 fusion.39
  118.0 1.8 convolution_convert_fusion.3
  119.9 1.6 convert_element_type.155
  121.6 25.3 %reduce-scatter.11.cloned.1.call-done = bf16[256,768]{1,0:T(8,128)(2,1)} async-done(((bf16[1024,768]{1,0:T(8,128)(2,1)}), bf16[256,768]{1,0:T(8,128)(2,1)}) %reduce-scatter.11.cloned.1.call-update) | async-done | bytes 393232 | tf_op jit(solution)/shard_map/reduce_scatter | solution.py:206
  146.9 1.3 fusion.69
  148.8 2.0 add_convert_fusion.1
  150.9 1.6 convert_element_type.157
  152.6 18.5 %all_to_all.34 = bf16[8,32,768]{2,1,0:T(8,128)(2,1)} all-to-all(bf16[8,32,768]{2,1,0:T(8,128)(2,1)} %get-tuple-element.120), channel_id=1, replica_groups=mesh['dp'=8,'tensor'=4] {'dp'}, dimensions={0} | all-to-all | bytes 786432 | tf_op jit(solution)/shard_map/all_to_all | solution.py:166
  171.4 14.1 %all-gather.9.cloned.1.call-done = bf16[1024,768]{1,0:T(8,128)(2,1)} async-done(((bf16[256,768]{1,0:T(8,128)(2,1)}), bf16[1024,768]{1,0:T(8,128)(2,1)}) %all-gather.9.cloned.1.call-update) | async-done | bytes 1572880 | tf_op jit(solution)/shard_map/all_gather | solution.py:211
  185.5 4.9 fusion.83
  190.4 39.0 %all-gather.13.cloned.1.call-done = bf16[768,768]{0,1:T(8,128)(2,1)} async-done(((bf16[768,96]{0,1:T(8,128)(2,1)}), bf16[768,768]{0,1:T(8,128)(2,1)}) %all-gather.13.cloned.1.call-update) | async-done | bytes 1179664 | tf_op jit(solution)/shard_map/all_gather | solution.py:179
  229.3 19.7 %all-gather.15.cloned.1.call-done = bf16[1024,768]{1,0:T(8,128)(2,1)} async-done(((bf16[256,768]{1,0:T(8,128)(2,1)}), bf16[1024,768]{1,0:T(8,128)(2,1)}) %all-gather.15.cloned.1.call-update) | async-done | bytes 1572880 | tf_op jit(solution)/shard_map/all_gather | solution.py:49
  249.0 6.9 %convert_reduce_fusion = (f32[768]{0:T(1024)}, bf16[1024,768]{1,0:T(8,128)(2,1)S(1)}) fusion(f32[1024,768]{1,0:T(8,128)} %fusion.83, f32[768]{0:T(1024)} %param.43, bf16[1024,768]{1,0:T(8,128)(2,1)} %all-gather.15.cloned.1.call-done, bf16[768,768]{0,1:T(8,128)(2,1)} %all-gather.13.cloned.1.call-done), kind=kOutput, calls=%fused_computation.23 | convolution fusion | flops 1229192448 | bytes 7477248 | tf_op jit(solution)/shard_map/dot_general | solution.py:20
  255.9 1.2 copy-done.58
  257.1 2.6 convolution_convert_fusion.1
  259.7 5.5 convolution_convert_fusion.2
  265.3 22.7 %reduce-scatter.15.cloned.1.call-done = bf16[256,768]{1,0:T(8,128)(2,1)} async-done(((bf16[1024,768]{1,0:T(8,128)(2,1)}), bf16[256,768]{1,0:T(8,128)(2,1)}) %reduce-scatter.15.cloned.1.call-update) | async-done | bytes 393232 | tf_op jit(solution)/shard_map/reduce_scatter | solution.py:53
  288.0 2.3 fusion.57
  291.4 27.2 %reduce-scatter.13.cloned.1.call-done = bf16[256,768]{1,0:T(8,128)(2,1)} async-done(((bf16[1024,768]{1,0:T(8,128)(2,1)}), bf16[256,768]{1,0:T(8,128)(2,1)}) %reduce-scatter.13.cloned.1.call-update) | async-done | bytes 393232 | tf_op jit(solution)/shard_map/reduce_scatter | solution.py:214
  318.6 3.3 fusion.74
  321.9 0.9 copy-done.3
  322.8 0.8 convert_element_type.165
  325.3 17.9 %all-gather.17.cloned.1.call-done = bf16[1024,768]{1,0:T(8,128)(2,1)} async-done(((bf16[256,768]{1,0:T(8,128)(2,1)}), bf16[1024,768]{1,0:T(8,128)(2,1)}) %all-gather.17.cloned.1.call-update) | async-done | bytes 1572880 | tf_op jit(solution)/shard_map/all_gather | solution.py:49
  343.2 2.2 convolution_convert_fusion.4
  346.8 0.9 multiply_convert_fusion.1
  350.1 1.9 multiply_reduce_fusion
  352.0 1.3 convert_reduce_fusion.5
  353.2 1.4 multiply_convert_fusion
  354.7 1.1 fusion.35
  357.4 2.6 convolution_convert_fusion
  360.0 1.6 convolution_bitcast_fusion
  361.7 5.6 fusion.72
  367.7 5.1 fusion.84
  373.0 2.4 fusion.68
  375.4 3.1 copy.64
  378.5 5.7 all-to-all-start.1
  384.2 4.0 reduce-scatter.17.cloned.1.call-done
  388.2 1.4 fusion.58
  389.7 2.1 fusion.51
  391.8 4.5 all-to-all-done.1
  396.3 3.6 all-to-all-start.3
  400.8 23.4 %all-reduce.3 = (f32[2,192]{1,0:T(2,128)}, f32[768]{0:T(1024)}) all-reduce(f32[2,192]{1,0:T(2,128)S(1)} %pad_maximum_fusion.4, f32[768]{0:T(1024)S(1)} %copy-done.52), channel_id=1, replica_groups=mesh['dp'=8,'tensor'=4] {'dp'}, use_global_device_ids=true, to_apply=%region_28.30 | all-reduce | flops 1152 | bytes 9216 | tf_op jit(solution)/shard_map/psum | solution.py:278
  424.3 30.8 %reduce-scatter.25.cloned.1.call-done = f32[96,192]{1,0:T(8,128)} async-done(((f32[768,192]{1,0:T(8,128)}), f32[96,192]{1,0:T(8,128)}) %reduce-scatter.25.cloned.1.call-update) | async-done | bytes 73744
  455.1 1.6 copy.70
  456.7 41.3 %all-reduce.2 = (f32[768]{0:T(1024)}, f32[768]{0:T(1024)}, f32[768]{0:T(1024)}, f32[768]{0:T(1024)}, f32[768]{0:T(1024)}, /*index=5*/f32[768]{0:T(1024)}) all-reduce(f32[768]{0:T(1024)S(1)} %get-tuple-element.83, f32[768]{0:T(1024)S(1)} %get-tuple-element.88, ...), channel_id=1, replica_groups=mesh['dp'=8,'tensor'=4] {'dp','tensor'}, use_global_device_ids=true, to_apply=%region_22.24 | all-reduce | flops 4608 | bytes 36864 | tf_op jit(solution)/shard_map/psum | solution.py:279
  498.6 1.0 broadcast_select_fusion
  499.6 28.4 %reduce-scatter.23.cloned.1.call-done = f32[768,96]{0,1:T(8,128)} async-done(((f32[768,768]{0,1:T(8,128)}), f32[768,96]{0,1:T(8,128)}) %reduce-scatter.23.cloned.1.call-update) | async-done | bytes 294928 | tf_op jit(solution)/shard_map/reduce_scatter | solution.py:275
  527.9 72.4 %reduce-scatter.21.cloned.1.call-done = f32[96,768]{1,0:T(8,128)} async-done(((f32[768,768]{1,0:T(8,128)}), f32[96,768]{1,0:T(8,128)}) %reduce-scatter.21.cloned.1.call-update) | async-done | bytes 294928 | tf_op jit(solution)/shard_map/reduce_scatter | solution.py:274
  600.3 72.5 %reduce-scatter.19.cloned.1.call-done = f32[96,3,192]{2,0,1:T(8,128)} async-done(((f32[768,3,192]{2,0,1:T(8,128)}), f32[96,3,192]{2,0,1:T(8,128)}) %reduce-scatter.19.cloned.1.call-update) | async-done | bytes 221200 | tf_op jit(solution)/shard_map/reduce_scatter | solution.py:272
  (200 shorter events, 16.4 us)
Async XLA Ops:
  8.0 23.6 %copy-start.38 = (f32[768]{0:T(1024)S(1)}, f32[768]{0:T(1024)}, u32[]{:S(2)}) copy-start(f32[768]{0:T(1024)} %param.34) | copy-start | bytes 9220
  8.0 23.6 %copy-start.51 = (f32[768]{0:T(1024)S(1)}, f32[768]{0:T(1024)}, u32[]{:S(2)}) copy-start(f32[768]{0:T(1024)} %param.35) | copy-start | bytes 9220
  8.1 24.6 %copy-start.53 = (s32[8,4]{0,1:T(4,128)S(1)}, s32[8,4]{0,1:T(4,128)}, u32[]{:S(2)}) copy-start(s32[8,4]{0,1:T(4,128)} %param.32) | copy-start | bytes 388
  8.1 25.0 %copy-start.34 = (f32[192,96]{1,0:T(8,128)S(1)}, f32[192,96]{1,0:T(8,128)}, u32[]{:S(2)}) copy-start(f32[192,96]{1,0:T(8,128)} %param.38) | copy-start | bytes 221188
  8.1 25.1 %copy-start.33 = (f32[96,3,192]{2,0,1:T(8,128)S(1)}, f32[96,3,192]{2,0,1:T(8,128)}, u32[]{:S(2)}) copy-start(f32[96,3,192]{2,0,1:T(8,128)} %param.36) | copy-start | bytes 663556
  8.1 97.5 %all-gather.7.cloned.1.call-start = ((), (), s32[]{:S(2)}) async-start(), calls=%async_computation.12 | async-start | bytes 1966080 | tf_op jit(solution)/shard_map/all_gather | solution.py:186
  31.5 38.7 %copy-start.42 = (f32[256]{0:T(256)}, f32[256]{0:T(256)S(1)}, u32[]{:S(2)}) copy-start(f32[256]{0:T(256)S(1)} %div.45) | copy-start | bytes 3076
  31.6 38.6 %copy-start.44 = (f32[256]{0:T(256)}, f32[256]{0:T(256)S(1)}, u32[]{:S(2)}) copy-start(f32[256]{0:T(256)S(1)} %add_rsqrt_fusion.1) | copy-start | bytes 3076
  32.6 70.7 %copy-start.54 = (f32[2,192]{1,0:T(2,128)S(1)}, f32[2,192]{1,0:T(2,128)}, u32[]{:S(2)}) copy-start(f32[2,192]{1,0:T(2,128)} %param.37) | copy-start | bytes 4612
  32.6 114.3 %reduce-scatter.11.cloned.1.call-start = ((), (), s32[]{:S(2)}) async-start(), calls=%async_computation.13 | async-start | bytes 1966080 | tf_op jit(solution)/shard_map/reduce_scatter | solution.py:206
  70.2 37.9 %copy-start.9 = (bf16[768,3,192]{0,2,1:T(8,128)(2,1)}, bf16[768,3,192]{0,2,1:T(8,128)(2,1)S(1)}, u32[]{:S(2)}) copy-start(bf16[768,3,192]{0,2,1:T(8,128)(2,1)S(1)} %copy.58) | copy-start | bytes 2654212
  108.1 1.8 copy-start.22
  108.2 2.9 copy-start.7
  108.3 6.1 copy-start.15
  108.4 2.7 copy-start.17
  108.4 1.9 copy-start.25
  112.9 2.7 copy-start.2
  112.9 2.7 copy-start.35
  114.4 2.8 copy-start.41
  115.5 2.5 copy-start.11
  117.2 29.7 %copy-start.36 = (f32[768]{0:T(1024)S(1)}, f32[768]{0:T(1024)}, u32[]{:S(2)}) copy-start(f32[768]{0:T(1024)} %param.39) | copy-start | bytes 9220
  117.2 31.6 %copy-start.37 = (f32[768]{0:T(1024)S(1)}, f32[768]{0:T(1024)}, u32[]{:S(2)}) copy-start(f32[768]{0:T(1024)} %param.40) | copy-start | bytes 9220
  119.8 51.5 %all-gather.11.cloned.1.call-start = ((), (), s32[]{:S(2)}) async-start(), calls=%async_computation.15 | async-start | bytes 1327104 | tf_op jit(solution)/shard_map/all_gather | solution.py:178
  121.6 63.9 %all-gather.9.cloned.1.call-start = ((), (), s32[]{:S(2)}) async-start(), calls=%async_computation.14 | async-start | bytes 1966080 | tf_op jit(solution)/shard_map/all_gather | solution.py:211
  150.8 78.5 %all-gather.13.cloned.1.call-start = ((), (), s32[]{:S(2)}) async-start(), calls=%async_computation.16 | async-start | bytes 1327104 | tf_op jit(solution)/shard_map/all_gather | solution.py:179
  152.5 96.5 %all-gather.15.cloned.1.call-start = ((), (), s32[]{:S(2)}) async-start(), calls=%async_computation.18 | async-start | bytes 1966080 | tf_op jit(solution)/shard_map/all_gather | solution.py:49
  171.1 116.9 %reduce-scatter.15.cloned.1.call-start = ((), (), s32[]{:S(2)}) async-start(), calls=%async_computation.19 | async-start | bytes 1966080 | tf_op jit(solution)/shard_map/reduce_scatter | solution.py:53
  249.0 8.1 %copy-start.55 = (bf16[768,768]{1,0:T(8,128)(2,1)S(1)}, bf16[768,768]{1,0:T(8,128)(2,1)}, u32[]{:S(2)}) copy-start(bf16[768,768]{1,0:T(8,128)(2,1)} %all-gather.11.cloned.1.call-done) | copy-start | bytes 3538948
  255.9 1.2 copy-start.58
  259.7 58.9 %reduce-scatter.13.cloned.1.call-start = ((), (), s32[]{:S(2)}) async-start(), calls=%async_computation.17 | async-start | bytes 1966080 | tf_op jit(solution)/shard_map/reduce_scatter | solution.py:214
  265.3 77.9 %all-gather.17.cloned.1.call-start = ((), (), s32[]{:S(2)}) async-start(), calls=%async_computation.20 | async-start | bytes 1966080 | tf_op jit(solution)/shard_map/all_gather | solution.py:49
  323.6 64.6 %reduce-scatter.17.cloned.1.call-start = ((), (), s32[]{:S(2)}) async-start(), calls=%async_computation.21 | async-start | bytes 1966080 | tf_op jit(solution)/shard_map/reduce_scatter | solution.py:53
  343.2 2.8 copy-start.26
  346.8 2.4 slice-start
  346.8 1.5 copy-start.21
  346.8 3.0 slice-start.1
  347.9 2.2 copy-start.16
  353.2 3.4 copy-start.29
  353.2 1.4 copy-start.8
  355.7 1.6 copy-start.10
  357.3 2.7 copy-start.6
  357.3 2.7 copy-start.13
  359.9 1.8 copy-start.56
  360.0 95.1 %reduce-scatter.25.cloned.1.call-start = ((), (), s32[]{:S(2)}) async-start(), calls=%async_computation.25 | async-start | bytes 884736
  361.7 166.3 %reduce-scatter.23.cloned.1.call-start = ((), (), s32[]{:S(2)}) async-start(), calls=%async_computation.24 | async-start | bytes 2654208 | tf_op jit(solution)/shard_map/reduce_scatter | solution.py:275
  367.4 5.6 copy-start.14
  367.4 5.6 copy-start.28
  367.4 5.6 copy-start.30
  367.4 5.6 copy-start.32
  367.4 232.9 %reduce-scatter.21.cloned.1.call-start = ((), (), s32[]{:S(2)}) async-start(), calls=%async_computation.23 | async-start | bytes 2654208 | tf_op jit(solution)/shard_map/reduce_scatter | solution.py:274
  372.9 299.9 %reduce-scatter.19.cloned.1.call-start = ((), (), s32[]{:S(2)}) async-start(), calls=%async_computation.22 | async-start | bytes 2654208 | tf_op jit(solution)/shard_map/reduce_scatter | solution.py:272
  375.4 12.8 %copy-start.39 = (f32[768]{0:T(1024)S(1)}, f32[768]{0:T(1024)}, u32[]{:S(2)}) copy-start(f32[768]{0:T(1024)} %param.34) | copy-start | bytes 9220
  375.4 12.8 %copy-start.43 = (f32[256]{0:T(256)S(1)}, f32[256]{0:T(256)}, u32[]{:S(2)}) copy-start(f32[256]{0:T(256)} %copy-done.42) | copy-start | bytes 3076
  375.4 12.8 %copy-start.45 = (f32[256]{0:T(256)S(1)}, f32[256]{0:T(256)}, u32[]{:S(2)}) copy-start(f32[256]{0:T(256)} %copy-done.44) | copy-start | bytes 3076
  375.4 14.3 %copy-start.4 = (f32[256,768]{1,0:T(8,128)S(1)}, f32[256,768]{1,0:T(8,128)}, u32[]{:S(2)}) copy-start(f32[256,768]{1,0:T(8,128)} %copy-done.3) | copy-start | bytes 2359300
  378.4 21.5 %copy-start.57 = (s32[8]{0:T(128)S(1)}, s32[8]{0:T(128)}, u32[]{:S(2)}) copy-start(s32[8]{0:T(128)} %param.33) | copy-start | bytes 100
  378.4 21.5 %copy-start.5 = (bf16[8,32,768]{2,1,0:T(8,128)(2,1)S(1)}, bf16[8,32,768]{2,1,0:T(8,128)(2,1)}, u32[]{:S(2)}) copy-start(bf16[8,32,768]{2,1,0:T(8,128)(2,1)} %all_to_all.34) | copy-start | bytes 1179652
  378.5 22.4 %copy-start.52 = (f32[768]{0:T(1024)S(1)}, f32[768]{0:T(1024)}, u32[]{:S(2)}) copy-start(f32[768]{0:T(1024)} %get-tuple-element.99) | copy-start | bytes 9220
  378.5 78.2 %copy-start.48 = (f32[768]{0:T(1024)S(1)}, f32[768]{0:T(1024)}, u32[]{:S(2)}) copy-start(f32[768]{0:T(1024)} %get-tuple-element.79) | copy-start | bytes 9220
  378.5 78.2 %copy-start.49 = (f32[768]{0:T(1024)S(1)}, f32[768]{0:T(1024)}, u32[]{:S(2)}) copy-start(f32[768]{0:T(1024)} %get-tuple-element.87) | copy-start | bytes 9220
  378.5 78.2 %copy-start.50 = (f32[768]{0:T(1024)S(1)}, f32[768]{0:T(1024)}, u32[]{:S(2)}) copy-start(f32[768]{0:T(1024)} %get-tuple-element.103) | copy-start | bytes 9220
  378.5 17.8 %all-to-all-start.1 = ((bf16[8,32,768]{2,1,0:T(8,128)(2,1)}), bf16[8,32,768]{2,1,0:T(8,128)(2,1)S(1)}, u32[]{:S(2)}, u32[]{:S(2)}) async-start(bf16[8,32,768]{2,1,0:T(8,128)(2,1)} %bitcast.15), calls=%async_computation.3 | async-start | bytes 786432 | tf_op jit(solution)/shard_map/all_to_all | solution.py:262
  389.6 283.2 %copy-start.1 = (bf16[256,768]{1,0:T(8,128)(2,1)S(1)}, bf16[256,768]{1,0:T(8,128)(2,1)}, u32[]{:S(2)}) copy-start(bf16[256,768]{1,0:T(8,128)(2,1)} %param.31) | copy-start | bytes 1179652
  396.3 101.7 %all-to-all-start.3 = ((bf16[8,32,768]{2,1,0:T(8,128)(2,1)}), bf16[8,32,768]{2,1,0:T(8,128)(2,1)S(1)}, u32[]{:S(2)}, u32[]{:S(2)}) async-start(bf16[8,32,768]{2,1,0:T(8,128)(2,1)} %bitcast.30), calls=%async_computation.7 | async-start | bytes 786432 | tf_op jit(solution)/shard_map/all_to_all | solution.py:263
  (13 other events, 11.0 us)
Sparse Core Ops, SparseCore 0:
  32.8 18.3 all-gather.6
  120.0 26.9 reduce-scatter.10
  259.8 28.1 reduce-scatter.14
  290.4 28.1 reduce-scatter.12
Sparse Core Ops, SparseCore 1:
  123.3 41.1 all-gather.10
  166.5 18.9 all-gather.8
  187.8 41.5 all-gather.12
  231.0 18.0 all-gather.14
  323.7 19.5 all-gather.16
  360.0 28.1 reduce-scatter.16
  391.3 63.7 reduce-scatter.24
  459.4 68.5 reduce-scatter.22
  532.3 68.0 reduce-scatter.20
  604.8 67.9 reduce-scatter.18
where the time goes:
time: 681 us; the launch traced here: 680 us
  waiting for transfers between devices  379 us (56%)
  blocking collectives  171 us (25%)
  matrix products  55.5 us (8%)
  other arithmetic  30.1 us (4%)
  local copies, waits for them, and re-layouts  17.6 us (3%)
  between operations  16.2 us (2%)
  starting transfers between devices  10.6 us (2%)
    reduce_scatter x1, waiting for transfers between devices, local(): lax.psum_scatter(qkv_grad, 'dp', scatter_dimension=0, tiled=True)  72.5 us
    reduce_scatter x1, waiting for transfers between devices, local(): lax.psum_scatter(fc_grad, 'dp', scatter_dimension=0, tiled=True)  72.4 us
    psum x1, blocking collectives, local(): lax.psum((ln1_gain_grad, ln1_bias_grad, attn_out_bias_grad, ln2_gain_grad...  41.3 us
    all_gather x1, waiting for transfers between devices, local(): lax.all_gather(proj_weight.astype(jnp.bfloat16), 'dp', axis=1, tiled=True)  39 us
    all_gather x2, waiting for transfers between devices, grad_rows(): return lax.all_gather(local_rows, 'tensor', axis=0, tiled=True)  37.6 us
    all_gather x1, blocking collectives, local(): lax.all_gather(qkv_weight.astype(jnp.bfloat16), 'dp', axis=0, tiled=True)  36 us
    all_gather x1, blocking collectives, local(): lax.all_gather(attn_out_weight.astype(jnp.bfloat16), 'dp', axis=1, tiled=...  33 us
    unnamed x15, waiting for transfers between devices  31 us
  transfers between devices with their start and end apart: 16, of which 13 were waited for; matrix products, arithmetic and copies ran while one was open for 7% of the time, Pallas kernels for 0%

commit v1 on v0

--- a/solution.py
+++ b/solution.py
@@ -146,6 +146,24 @@
     proj_weight,
     proj_bias,
 ):
+
+    def lead_sites(my_data, axis_key):
+        far_arr = jax.lax.axis_size(axis_key)
+        r1 = jax.lax.axis_index(axis_key)
+        z_new, view_out = (far_arr, r1)
+        y1 = my_data.shape[0] // z_new
+        q_next = jnp.roll(my_data, -view_out * y1, 0)
+        store = [lax.slice_in_dim(q_next, 0, y1, axis=0)]
+        for k0 in [*range(1, z_new)]:
+            arr_out = lax.slice_in_dim(q_next, k0 * y1, (k0 + 1) * y1, axis=0)
+            store.append(
+                jax.lax.ppermute(
+                    arr_out, axis_key, [(at, (at + k0) % z_new) for at in range(z_new)]
+                )
+            )
+        value_now = jnp.concatenate(store[::-1], 0)
+        return jnp.roll(value_now, (view_out + 1) * store[0].shape[0], 0)
+
     local_rows, width = block_input.shape
     pack_count = pack_order.shape[0]
     piece_rows = local_rows // pack_count
@@ -162,7 +180,7 @@
         out_cotangent.reshape(pack_count, piece_rows, width), inverse, axis=0
     ).reshape(local_rows, width)
     arrived = (
-        lax.all_to_all(sent_input, "dp", split_axis=0, concat_axis=0, tiled=True),
+        lead_sites(sent_input, "dp"),
         lax.all_to_all(sent_grad, "dp", split_axis=0, concat_axis=0, tiled=True),
     )
     input_here = arrived[0].astype(jnp.float32)

time: 681 us -> 695 us (1.021); the launches traced: 680 us -> 686 us
  starting transfers between devices: 10.6 us -> 26.8 us
  blocking collectives: 171 us -> 155 us
    all_to_all x1 -> x0, blocking collectives: 19.1 us -> none  [local(): lax.all_to_all(sent_input, 'dp', split_axis=0, concat_axis=0, tiled=True)]
    ppermute x0 -> x7, starting transfers between devices: none -> 16 us  [lead_sites(): jax.lax.ppermute(arr_out, axis_key, [(at, (at + k0) % z_new) for at in ra...]
  transfers between devices with their start and end apart: 16 -> 23, of which waited for: 13 -> 15; matrix products, arithmetic and copies ran while one was open for 7% -> 7% of each run, Pallas kernels for 0% -> 0%
where the time goes in v1:
time: 695 us; the launch traced here: 686 us
  waiting for transfers between devices  384 us (55%)
  blocking collectives  155 us (22%)
  matrix products  55.5 us (8%)
  other arithmetic  30.6 us (4%)
  starting transfers between devices  26.8 us (4%)
  local copies, waits for them, and re-layouts  17.5 us (3%)
  between operations  16.6 us (2%)
    reduce_scatter x1, waiting for transfers between devices, local(): lax.psum_scatter(fc_grad, 'dp', scatter_dimension=0, tiled=True)  72.6 us
    reduce_scatter x1, waiting for transfers between devices, local(): lax.psum_scatter(qkv_grad, 'dp', scatter_dimension=0, tiled=True)  72.6 us
    psum x1, blocking collectives, local(): lax.psum((ln1_gain_grad, ln1_bias_grad, attn_out_bias_grad, ln2_gain_grad...  41.2 us
    all_gather x1, waiting for transfers between devices, local(): lax.all_gather(proj_weight.astype(jnp.bfloat16), 'dp', axis=1, tiled=True)  39 us
    all_gather x1, blocking collectives, local(): lax.all_gather(qkv_weight.astype(jnp.bfloat16), 'dp', axis=0, tiled=True)  38.6 us
    all_gather x2, waiting for transfers between devices, grad_rows(): return lax.all_gather(local_rows, 'tensor', axis=0, tiled=True)  37.6 us
    all_gather x1, blocking collectives, local(): lax.all_gather(attn_out_weight.astype(jnp.bfloat16), 'dp', axis=1, tiled=...  33 us
    unnamed x15, waiting for transfers between devices  30.8 us
  transfers between devices with their start and end apart: 23, of which 15 were waited for; matrix products, arithmetic and copies ran while one was open for 7% of the time, Pallas kernels for 0%

profile of v1, /device:TPU:0, one launch (start us, length us, event | category | flops | bytes accessed | tf_op | source)
XLA Modules:
  0.0 685.9 jit_solution(10482925746883633321)
XLA Ops:
  9.6 1.6 gather_fusion
  12.6 6.0 collective-permute-start
  18.6 2.5 collective-permute-start.4
  21.1 2.8 collective-permute-start.3
  23.9 2.9 collective-permute-start.1
  26.8 1.7 collective-permute-done.1
  28.6 1.8 collective-permute-start.2
  30.4 3.2 collective-permute-done.2
  34.1 1.0 fusion.63
  35.8 38.6 %all_gather.25 = bf16[768,3,192]{2,1,0:T(4,128)(2,1)S(1)} all-gather(bf16[96,3,192]{2,1,0:T(4,128)(2,1)S(1)} %copy.57), channel_id=1, replica_groups=mesh['dp'=8,'tensor'=4] {'dp'}, dimensions={0}, use_global_device_ids=true | all-gather | bytes 995328 | tf_op jit(solution)/shard_map/all_gather | solution.py:194
  75.4 33.0 %all_gather.26 = bf16[192,768]{0,1:T(8,128)(2,1)} all-gather(bf16[192,96]{0,1:T(8,128)(2,1)S(1)} %copy.60), channel_id=1, replica_groups=mesh['dp'=8,'tensor'=4] {'dp'}, dimensions={1}, use_global_device_ids=true | all-gather | bytes 331776 | tf_op jit(solution)/shard_map/all_gather | solution.py:195
  108.5 0.9 fusion.47
  109.4 1.3 fusion.14
  110.7 2.5 fusion.84
  116.5 1.5 fusion.85
  118.0 1.5 fusion
  119.5 1.1 copy-done.2
  120.7 1.6 fusion.39
  123.2 1.8 convolution_convert_fusion.3
  125.1 1.6 convert_element_type.146
  126.8 25.7 %reduce-scatter.11.cloned.1.call-done = bf16[256,768]{1,0:T(8,128)(2,1)} async-done(((bf16[1024,768]{1,0:T(8,128)(2,1)}), bf16[256,768]{1,0:T(8,128)(2,1)}) %reduce-scatter.11.cloned.1.call-update) | async-done | bytes 393232 | tf_op jit(solution)/shard_map/reduce_scatter | solution.py:224
  152.5 1.3 fusion.71
  154.3 2.0 add_convert_fusion.1
  156.4 1.6 convert_element_type.148
  158.1 18.5 %all_to_all.27 = bf16[8,32,768]{2,1,0:T(8,128)(2,1)} all-to-all(bf16[8,32,768]{2,1,0:T(8,128)(2,1)} %get-tuple-element.131), channel_id=1, replica_groups=mesh['dp'=8,'tensor'=4] {'dp'}, dimensions={0} | all-to-all | bytes 786432 | tf_op jit(solution)/shard_map/all_to_all | solution.py:184
  177.2 13.9 %all-gather.9.cloned.1.call-done = bf16[1024,768]{1,0:T(8,128)(2,1)} async-done(((bf16[256,768]{1,0:T(8,128)(2,1)}), bf16[1024,768]{1,0:T(8,128)(2,1)}) %all-gather.9.cloned.1.call-update) | async-done | bytes 1572880 | tf_op jit(solution)/shard_map/all_gather | solution.py:229
  191.1 4.8 fusion.87
  195.9 39.0 %all-gather.13.cloned.1.call-done = bf16[768,768]{0,1:T(8,128)(2,1)} async-done(((bf16[768,96]{0,1:T(8,128)(2,1)}), bf16[768,768]{0,1:T(8,128)(2,1)}) %all-gather.13.cloned.1.call-update) | async-done | bytes 1179664 | tf_op jit(solution)/shard_map/all_gather | solution.py:197
  234.9 19.7 %all-gather.15.cloned.1.call-done = bf16[1024,768]{1,0:T(8,128)(2,1)} async-done(((bf16[256,768]{1,0:T(8,128)(2,1)}), bf16[1024,768]{1,0:T(8,128)(2,1)}) %all-gather.15.cloned.1.call-update) | async-done | bytes 1572880 | tf_op jit(solution)/shard_map/all_gather | solution.py:49
  254.6 6.9 %convert_reduce_fusion = (f32[768]{0:T(1024)}, bf16[1024,768]{1,0:T(8,128)(2,1)S(1)}) fusion(f32[1024,768]{1,0:T(8,128)} %fusion.87, f32[768]{0:T(1024)} %param.45, bf16[1024,768]{1,0:T(8,128)(2,1)} %all-gather.15.cloned.1.call-done, bf16[768,768]{0,1:T(8,128)(2,1)} %all-gather.13.cloned.1.call-done), kind=kOutput, calls=%fused_computation.23 | convolution fusion | flops 1229192448 | bytes 7477248 | tf_op jit(solution)/shard_map/dot_general | solution.py:20
  261.5 1.2 copy-done.58
  262.7 2.6 convolution_convert_fusion.1
  265.3 5.5 convolution_convert_fusion.2
  270.9 22.7 %reduce-scatter.15.cloned.1.call-done = bf16[256,768]{1,0:T(8,128)(2,1)} async-done(((bf16[1024,768]{1,0:T(8,128)(2,1)}), bf16[256,768]{1,0:T(8,128)(2,1)}) %reduce-scatter.15.cloned.1.call-update) | async-done | bytes 393232 | tf_op jit(solution)/shard_map/reduce_scatter | solution.py:53
  293.6 2.3 fusion.57
  297.0 27.2 %reduce-scatter.13.cloned.1.call-done = bf16[256,768]{1,0:T(8,128)(2,1)} async-done(((bf16[1024,768]{1,0:T(8,128)(2,1)}), bf16[256,768]{1,0:T(8,128)(2,1)}) %reduce-scatter.13.cloned.1.call-update) | async-done | bytes 393232 | tf_op jit(solution)/shard_map/reduce_scatter | solution.py:232
  324.2 3.3 fusion.76
  327.4 0.9 copy-done.3
  330.8 18.0 %all-gather.17.cloned.1.call-done = bf16[1024,768]{1,0:T(8,128)(2,1)} async-done(((bf16[256,768]{1,0:T(8,128)(2,1)}), bf16[1024,768]{1,0:T(8,128)(2,1)}) %all-gather.17.cloned.1.call-update) | async-done | bytes 1572880 | tf_op jit(solution)/shard_map/all_gather | solution.py:49
  348.8 2.2 convolution_convert_fusion.4
  355.6 1.9 multiply_reduce_fusion
  357.6 1.3 convert_reduce_fusion.5
  358.8 1.4 multiply_convert_fusion
  360.2 1.1 fusion.35
  362.9 2.6 convolution_convert_fusion
  365.6 1.7 convolution_bitcast_fusion
  367.4 5.6 fusion.74
  373.3 5.1 fusion.88
  378.5 2.4 fusion.68
  380.9 3.1 copy.64
  384.1 5.7 all-to-all-start
  389.8 4.0 reduce-scatter.17.cloned.1.call-done
  393.7 1.4 fusion.58
  395.2 2.1 fusion.51
  397.3 4.5 all-to-all-done
  401.9 3.6 all-to-all-start.2
  406.4 23.5 %all-reduce.3 = (f32[2,192]{1,0:T(2,128)}, f32[768]{0:T(1024)}) all-reduce(f32[2,192]{1,0:T(2,128)S(1)} %pad_maximum_fusion.4, f32[768]{0:T(1024)S(1)} %copy-done.52), channel_id=1, replica_groups=mesh['dp'=8,'tensor'=4] {'dp'}, use_global_device_ids=true, to_apply=%region_28.31 | all-reduce | flops 1152 | bytes 9216 | tf_op jit(solution)/shard_map/psum | solution.py:296
  429.9 30.6 %reduce-scatter.25.cloned.1.call-done = f32[96,192]{1,0:T(8,128)} async-done(((f32[768,192]{1,0:T(8,128)}), f32[96,192]{1,0:T(8,128)}) %reduce-scatter.25.cloned.1.call-update) | async-done | bytes 73744
  460.5 1.6 copy.70
  462.2 41.2 %all-reduce.2 = (f32[768]{0:T(1024)}, f32[768]{0:T(1024)}, f32[768]{0:T(1024)}, f32[768]{0:T(1024)}, f32[768]{0:T(1024)}, /*index=5*/f32[768]{0:T(1024)}) all-reduce(f32[768]{0:T(1024)S(1)} %get-tuple-element.84, f32[768]{0:T(1024)S(1)} %get-tuple-element.89, ...), channel_id=1, replica_groups=mesh['dp'=8,'tensor'=4] {'dp','tensor'}, use_global_device_ids=true, to_apply=%region_22.25 | all-reduce | flops 4608 | bytes 36864 | tf_op jit(solution)/shard_map/psum | solution.py:297
  504.0 1.0 broadcast_select_fusion
  505.0 28.4 %reduce-scatter.23.cloned.1.call-done = f32[768,96]{0,1:T(8,128)} async-done(((f32[768,768]{0,1:T(8,128)}), f32[768,96]{0,1:T(8,128)}) %reduce-scatter.23.cloned.1.call-update) | async-done | bytes 294928 | tf_op jit(solution)/shard_map/reduce_scatter | solution.py:293
  533.4 72.6 %reduce-scatter.21.cloned.1.call-done = f32[96,768]{1,0:T(8,128)} async-done(((f32[768,768]{1,0:T(8,128)}), f32[96,768]{1,0:T(8,128)}) %reduce-scatter.21.cloned.1.call-update) | async-done | bytes 294928 | tf_op jit(solution)/shard_map/reduce_scatter | solution.py:292
  606.0 72.6 %reduce-scatter.19.cloned.1.call-done = f32[96,3,192]{2,0,1:T(8,128)} async-done(((f32[768,3,192]{2,0,1:T(8,128)}), f32[96,3,192]{2,0,1:T(8,128)}) %reduce-scatter.19.cloned.1.call-update) | async-done | bytes 221200 | tf_op jit(solution)/shard_map/reduce_scatter | solution.py:290
  (219 shorter events, 22.2 us)
Async XLA Ops:
  8.0 102.7 %all-gather.7.cloned.1.call-start = ((), (), s32[]{:S(2)}) async-start(), calls=%async_computation.11 | async-start | bytes 1966080 | tf_op jit(solution)/shard_map/all_gather | solution.py:204
  8.1 26.0 %copy-start.38 = (f32[768]{0:T(1024)S(1)}, f32[768]{0:T(1024)}, u32[]{:S(2)}) copy-start(f32[768]{0:T(1024)} %param.36) | copy-start | bytes 9220
  8.1 26.0 %copy-start.51 = (f32[768]{0:T(1024)S(1)}, f32[768]{0:T(1024)}, u32[]{:S(2)}) copy-start(f32[768]{0:T(1024)} %param.37) | copy-start | bytes 9220
  9.6 25.6 %copy-start.53 = (s32[8,4]{0,1:T(4,128)S(1)}, s32[8,4]{0,1:T(4,128)}, u32[]{:S(2)}) copy-start(s32[8,4]{0,1:T(4,128)} %param.34) | copy-start | bytes 388
  9.6 26.0 %copy-start.34 = (f32[192,96]{1,0:T(8,128)S(1)}, f32[192,96]{1,0:T(8,128)}, u32[]{:S(2)}) copy-start(f32[192,96]{1,0:T(8,128)} %param.40) | copy-start | bytes 221188
  11.2 24.4 %copy-start.33 = (f32[96,3,192]{2,0,1:T(8,128)S(1)}, f32[96,3,192]{2,0,1:T(8,128)}, u32[]{:S(2)}) copy-start(f32[96,3,192]{2,0,1:T(8,128)} %param.38) | copy-start | bytes 663556
  12.6 11.3 %collective-permute-start = (bf16[32,768]{1,0:T(8,128)(2,1)S(1)}, bf16[32,768]{1,0:T(8,128)(2,1)S(1)}, u32[]{:S(2)}, u32[]{:S(2)}) collective-permute-start(bf16[32,768]{1,0:T(8,128)(2,1)S(1)} %get-tuple-element.120), channel_id=1, source_target_pairs={{0,28},{4,0},{8,4},{12,8},{16,12},{20,16},{24,20},{28,24},{1,29},{... | collective-permute-start | bytes 147464 | tf_op jit(solution)/shard_map/ppermute | solution.py:160
  18.6 15.0 %collective-permute-start.6 = (bf16[32,768]{1,0:T(8,128)(2,1)S(1)}, bf16[32,768]{1,0:T(8,128)(2,1)S(1)}, u32[]{:S(2)}, u32[]{:S(2)}) collective-permute-start(bf16[32,768]{1,0:T(8,128)(2,1)S(1)} %get-tuple-element.114), channel_id=1, source_target_pairs={{0,4},{4,8},{8,12},{12,16},{16,20},{20,24},{24,28},{28,0},{1,5},{5... | collective-permute-start | bytes 147464 | tf_op jit(solution)/shard_map/ppermute | solution.py:160
  18.6 15.0 %collective-permute-start.5 = (bf16[32,768]{1,0:T(8,128)(2,1)S(1)}, bf16[32,768]{1,0:T(8,128)(2,1)S(1)}, u32[]{:S(2)}, u32[]{:S(2)}) collective-permute-start(bf16[32,768]{1,0:T(8,128)(2,1)S(1)} %get-tuple-element.115), channel_id=1, source_target_pairs={{0,8},{4,12},{8,16},{12,20},{16,24},{20,28},{24,0},{28,4},{1,9},{5... | collective-permute-start | bytes 147464 | tf_op jit(solution)/shard_map/ppermute | solution.py:160
  18.6 15.0 %collective-permute-start.4 = (bf16[32,768]{1,0:T(8,128)(2,1)S(1)}, bf16[32,768]{1,0:T(8,128)(2,1)S(1)}, u32[]{:S(2)}, u32[]{:S(2)}) collective-permute-start(bf16[32,768]{1,0:T(8,128)(2,1)S(1)} %get-tuple-element.116), channel_id=1, source_target_pairs={{0,12},{4,16},{8,20},{12,24},{16,28},{20,0},{24,4},{28,8},{1,13},{... | collective-permute-start | bytes 147464 | tf_op jit(solution)/shard_map/ppermute | solution.py:160
  21.1 12.5 %collective-permute-start.3 = (bf16[32,768]{1,0:T(8,128)(2,1)S(1)}, bf16[32,768]{1,0:T(8,128)(2,1)S(1)}, u32[]{:S(2)}, u32[]{:S(2)}) collective-permute-start(bf16[32,768]{1,0:T(8,128)(2,1)S(1)} %get-tuple-element.117), channel_id=1, source_target_pairs={{0,16},{4,20},{8,24},{12,28},{16,0},{20,4},{24,8},{28,12},{1,17},{... | collective-permute-start | bytes 147464 | tf_op jit(solution)/shard_map/ppermute | solution.py:160
  23.9 4.7 collective-permute-start.1
  28.6 5.0 collective-permute-start.2
  34.1 41.2 %copy-start.42 = (f32[256]{0:T(256)}, f32[256]{0:T(256)S(1)}, u32[]{:S(2)}) copy-start(f32[256]{0:T(256)S(1)} %get-tuple-element.127) | copy-start | bytes 3076
  34.1 41.2 %copy-start.44 = (f32[256]{0:T(256)}, f32[256]{0:T(256)S(1)}, u32[]{:S(2)}) copy-start(f32[256]{0:T(256)S(1)} %get-tuple-element.128) | copy-start | bytes 3076
  35.1 73.3 %copy-start.54 = (f32[2,192]{1,0:T(2,128)S(1)}, f32[2,192]{1,0:T(2,128)}, u32[]{:S(2)}) copy-start(f32[2,192]{1,0:T(2,128)} %param.39) | copy-start | bytes 4612
  35.1 117.3 %reduce-scatter.11.cloned.1.call-start = ((), (), s32[]{:S(2)}) async-start(), calls=%async_computation.12 | async-start | bytes 1966080 | tf_op jit(solution)/shard_map/reduce_scatter | solution.py:224
  75.3 37.9 %copy-start.9 = (bf16[768,3,192]{0,2,1:T(8,128)(2,1)}, bf16[768,3,192]{0,2,1:T(8,128)(2,1)S(1)}, u32[]{:S(2)}) copy-start(bf16[768,3,192]{0,2,1:T(8,128)(2,1)S(1)} %copy.58) | copy-start | bytes 2654212
  113.3 2.9 copy-start.7
  113.5 6.1 copy-start.15
  113.5 2.7 copy-start.17
  118.0 2.6 copy-start.2
  118.0 2.7 copy-start.35
  119.5 2.8 copy-start.41
  120.7 2.5 copy-start.11
  122.3 30.1 %copy-start.36 = (f32[768]{0:T(1024)S(1)}, f32[768]{0:T(1024)}, u32[]{:S(2)}) copy-start(f32[768]{0:T(1024)} %param.41) | copy-start | bytes 9220
  122.4 32.0 %copy-start.37 = (f32[768]{0:T(1024)S(1)}, f32[768]{0:T(1024)}, u32[]{:S(2)}) copy-start(f32[768]{0:T(1024)} %param.42) | copy-start | bytes 9220
  125.0 52.2 %all-gather.11.cloned.1.call-start = ((), (), s32[]{:S(2)}) async-start(), calls=%async_computation.14 | async-start | bytes 1327104 | tf_op jit(solution)/shard_map/all_gather | solution.py:196
  126.7 64.3 %all-gather.9.cloned.1.call-start = ((), (), s32[]{:S(2)}) async-start(), calls=%async_computation.13 | async-start | bytes 1966080 | tf_op jit(solution)/shard_map/all_gather | solution.py:229
  156.4 78.6 %all-gather.13.cloned.1.call-start = ((), (), s32[]{:S(2)}) async-start(), calls=%async_computation.15 | async-start | bytes 1327104 | tf_op jit(solution)/shard_map/all_gather | solution.py:197
  158.1 96.5 %all-gather.15.cloned.1.call-start = ((), (), s32[]{:S(2)}) async-start(), calls=%async_computation.17 | async-start | bytes 1966080 | tf_op jit(solution)/shard_map/all_gather | solution.py:49
  176.7 116.9 %reduce-scatter.15.cloned.1.call-start = ((), (), s32[]{:S(2)}) async-start(), calls=%async_computation.18 | async-start | bytes 1966080 | tf_op jit(solution)/shard_map/reduce_scatter | solution.py:53
  254.6 8.1 %copy-start.55 = (bf16[768,768]{1,0:T(8,128)(2,1)S(1)}, bf16[768,768]{1,0:T(8,128)(2,1)}, u32[]{:S(2)}) copy-start(bf16[768,768]{1,0:T(8,128)(2,1)} %all-gather.11.cloned.1.call-done) | copy-start | bytes 3538948
  265.3 58.9 %reduce-scatter.13.cloned.1.call-start = ((), (), s32[]{:S(2)}) async-start(), calls=%async_computation.16 | async-start | bytes 1966080 | tf_op jit(solution)/shard_map/reduce_scatter | solution.py:232
  270.9 77.9 %all-gather.17.cloned.1.call-start = ((), (), s32[]{:S(2)}) async-start(), calls=%async_computation.19 | async-start | bytes 1966080 | tf_op jit(solution)/shard_map/all_gather | solution.py:49
  329.2 64.6 %reduce-scatter.17.cloned.1.call-start = ((), (), s32[]{:S(2)}) async-start(), calls=%async_computation.20 | async-start | bytes 1966080 | tf_op jit(solution)/shard_map/reduce_scatter | solution.py:53
  348.8 2.8 copy-start.26
  352.4 2.4 slice-start
  352.4 3.0 slice-start.1
  353.5 2.2 copy-start.16
  358.8 3.4 copy-start.29
  362.9 2.7 copy-start.6
  362.9 2.7 copy-start.13
  365.6 95.0 %reduce-scatter.25.cloned.1.call-start = ((), (), s32[]{:S(2)}) async-start(), calls=%async_computation.24 | async-start | bytes 884736
  367.3 166.1 %reduce-scatter.23.cloned.1.call-start = ((), (), s32[]{:S(2)}) async-start(), calls=%async_computation.23 | async-start | bytes 2654208 | tf_op jit(solution)/shard_map/reduce_scatter | solution.py:293
  373.0 5.5 copy-start.14
  373.0 5.5 copy-start.28
  373.0 5.5 copy-start.30
  373.0 5.5 copy-start.32
  373.0 232.9 %reduce-scatter.21.cloned.1.call-start = ((), (), s32[]{:S(2)}) async-start(), calls=%async_computation.22 | async-start | bytes 2654208 | tf_op jit(solution)/shard_map/reduce_scatter | solution.py:292
  378.4 300.1 %reduce-scatter.19.cloned.1.call-start = ((), (), s32[]{:S(2)}) async-start(), calls=%async_computation.21 | async-start | bytes 2654208 | tf_op jit(solution)/shard_map/reduce_scatter | solution.py:290
  380.9 12.9 %copy-start.39 = (f32[768]{0:T(1024)S(1)}, f32[768]{0:T(1024)}, u32[]{:S(2)}) copy-start(f32[768]{0:T(1024)} %param.36) | copy-start | bytes 9220
  380.9 12.9 %copy-start.43 = (f32[256]{0:T(256)S(1)}, f32[256]{0:T(256)}, u32[]{:S(2)}) copy-start(f32[256]{0:T(256)} %copy-done.42) | copy-start | bytes 3076
  380.9 12.9 %copy-start.45 = (f32[256]{0:T(256)S(1)}, f32[256]{0:T(256)}, u32[]{:S(2)}) copy-start(f32[256]{0:T(256)} %copy-done.44) | copy-start | bytes 3076
  380.9 14.3 %copy-start.4 = (f32[256,768]{1,0:T(8,128)S(1)}, f32[256,768]{1,0:T(8,128)}, u32[]{:S(2)}) copy-start(f32[256,768]{1,0:T(8,128)} %copy-done.3) | copy-start | bytes 2359300
  384.0 21.5 %copy-start.57 = (s32[8]{0:T(128)S(1)}, s32[8]{0:T(128)}, u32[]{:S(2)}) copy-start(s32[8]{0:T(128)} %param.35) | copy-start | bytes 100
  384.0 21.6 %copy-start.5 = (bf16[8,32,768]{2,1,0:T(8,128)(2,1)S(1)}, bf16[8,32,768]{2,1,0:T(8,128)(2,1)}, u32[]{:S(2)}) copy-start(bf16[8,32,768]{2,1,0:T(8,128)(2,1)} %all_to_all.27) | copy-start | bytes 1179652
  384.0 22.4 %copy-start.52 = (f32[768]{0:T(1024)S(1)}, f32[768]{0:T(1024)}, u32[]{:S(2)}) copy-start(f32[768]{0:T(1024)} %get-tuple-element.100) | copy-start | bytes 9220
  384.0 78.1 %copy-start.48 = (f32[768]{0:T(1024)S(1)}, f32[768]{0:T(1024)}, u32[]{:S(2)}) copy-start(f32[768]{0:T(1024)} %get-tuple-element.80) | copy-start | bytes 9220
  384.0 78.1 %copy-start.49 = (f32[768]{0:T(1024)S(1)}, f32[768]{0:T(1024)}, u32[]{:S(2)}) copy-start(f32[768]{0:T(1024)} %get-tuple-element.88) | copy-start | bytes 9220
  384.0 78.1 %copy-start.50 = (f32[768]{0:T(1024)S(1)}, f32[768]{0:T(1024)}, u32[]{:S(2)}) copy-start(f32[768]{0:T(1024)} %get-tuple-element.104) | copy-start | bytes 9220
  384.1 17.8 %all-to-all-start = ((bf16[8,32,768]{2,1,0:T(8,128)(2,1)}), bf16[8,32,768]{2,1,0:T(8,128)(2,1)S(1)}, u32[]{:S(2)}, u32[]{:S(2)}) async-start(bf16[8,32,768]{2,1,0:T(8,128)(2,1)} %bitcast.15), calls=%async_computation.2 | async-start | bytes 786432 | tf_op jit(solution)/shard_map/all_to_all | solution.py:280
  395.2 283.4 %copy-start.1 = (bf16[256,768]{1,0:T(8,128)(2,1)S(1)}, bf16[256,768]{1,0:T(8,128)(2,1)}, u32[]{:S(2)}) copy-start(bf16[256,768]{1,0:T(8,128)(2,1)} %param.33) | copy-start | bytes 1179652
  401.9 101.5 %all-to-all-start.2 = ((bf16[8,32,768]{2,1,0:T(8,128)(2,1)}), bf16[8,32,768]{2,1,0:T(8,128)(2,1)S(1)}, u32[]{:S(2)}, u32[]{:S(2)}) async-start(bf16[8,32,768]{2,1,0:T(8,128)(2,1)} %bitcast.30), calls=%async_computation.6 | async-start | bytes 786432 | tf_op jit(solution)/shard_map/all_to_all | solution.py:281
  (20 other events, 22.2 us)
Sparse Core Ops, SparseCore 0:
  35.3 22.3 all-gather.6
  125.1 27.2 reduce-scatter.10
  265.4 28.1 reduce-scatter.14
  296.0 28.1 reduce-scatter.12
Sparse Core Ops, SparseCore 1:
  128.5 41.5 all-gather.10
  172.1 18.9 all-gather.8
  193.4 41.5 all-gather.12
  236.6 18.0 all-gather.14
  329.2 19.5 all-gather.16
  365.6 28.0 reduce-scatter.16
  396.9 63.6 reduce-scatter.24
  464.9 68.5 reduce-scatter.22
  537.8 68.2 reduce-scatter.20
  610.5 68.0 reduce-scatter.18
